TPU v7x, 32 devices: a whole 2x2x4 slice. The times are simulated.
32 devices in a mesh: band: 8 (over z, y), grid: 4 (over x, core).
Axes of the slice: x: 2, y: 2, z: 4, core: 2. Of those that a mesh axis runs over, the one named last changes fastest.
Arguments:
- orbitals: bfloat16 [512, 64, 4096], P('band', 'grid'), may hold values from -6 to 6
- picks: int32 [1], replicated, may hold values from 0 to 511
Outputs:
- exchange_vectors: bfloat16 [512, 64, 4096], P('band', 'grid')
- gram: float32 [512, 512], P('band')
All inputs are finite; a program needn't handle non-finite values.
Results may differ from a plain program's by a relative error of at most 0.00085.
Values may be sent and summed in bfloat16 or wider, within the bound.
A program may use at most 192 MiB of HBM per device.

v0:
```python
import math

import jax
import jax.numpy as jnp
from jax import lax
from jax.sharding import PartitionSpec as P

NG = 64
NPTS = 262144


KERNEL_SCALE = 128.0
HIGHEST = lax.Precision.HIGHEST


def spread(value, axis, source):
    kept = jnp.where(lax.axis_index(axis) == source, value, 0).astype(value.dtype)
    return lax.psum(kept, axis)


def cas_matrix(length):
    products = (
        jnp.arange(length, dtype=jnp.int32)[:, None]
        * jnp.arange(length, dtype=jnp.int32)[None, :]
        % length
    )
    angles = products.astype(jnp.float32) * (2.0 * math.pi / length)
    return jnp.cos(angles) + jnp.sin(angles)


def folded_squares(first, length):
    frequency = first + jnp.arange(length, dtype=jnp.int32)
    folded = jnp.minimum(frequency, NG - frequency).astype(jnp.float32)
    return folded * folded


def transform_planes(field, matrix):
    batch, planes, square = field.shape
    shaped = field.reshape(batch, planes, NG, NG)
    shaped = jnp.einsum("bxyz,zk->bxyk", shaped, matrix, precision=HIGHEST)
    shaped = jnp.einsum("bxyz,yk->bxkz", shaped, matrix, precision=HIGHEST)
    return shaped.reshape(batch, planes, square)


def solve_potential(density):
    matrix = cas_matrix(NG)
    slab_rows = NG // lax.axis_size("grid")
    squares_first = folded_squares(0, NG)
    squares_second = folded_squares(lax.axis_index("grid") * slab_rows, slab_rows)
    summed = (
        squares_first[:, None, None] + squares_second[None, :, None] + squares_first[None, None, :]
    )
    table = jnp.where(summed > 0, KERNEL_SCALE / NPTS / jnp.maximum(summed, 1.0), 0.0)
    table = table.reshape(NG, slab_rows * NG)
    spectral = transform_planes(density, matrix)
    moved = jnp.einsum(
        "bxq,xk->bkq",
        lax.all_to_all(spectral, "grid", split_axis=2, concat_axis=1, tiled=True),
        matrix,
        precision=HIGHEST,
    )
    moved = moved * table[None]
    moved = jnp.einsum("bxq,xk->bkq", moved, matrix, precision=HIGHEST)
    slabs = lax.all_to_all(moved, "grid", split_axis=1, concat_axis=2, tiled=True)
    return transform_planes(slabs, matrix)


def apply_exchange(values, partners, solver):
    accumulated = jnp.zeros(values.shape, jnp.float32)
    partner = partners[0]
    potential = solver(values * partner[None])
    accumulated = accumulated - potential * partner[None]
    return accumulated.astype(jnp.bfloat16)


def per_device(orbitals, picks):
    local_bands = orbitals.shape[0]
    target = picks[0]
    owner = target // local_bands
    offset = target % local_bands
    mine = lax.dynamic_index_in_dim(orbitals, offset, 0, keepdims=False)
    partners = [spread(mine, "band", owner).astype(jnp.float32)]
    vectors = apply_exchange(orbitals.astype(jnp.float32), partners, solve_potential)
    flat_orbitals = orbitals.reshape(local_bands, -1)
    flat_vectors = vectors.reshape(local_bands, -1)
    spread_orbitals, spread_vectors = (
        lax.all_to_all(flat_orbitals, "band", split_axis=1, concat_axis=0, tiled=True),
        lax.all_to_all(flat_vectors, "band", split_axis=1, concat_axis=0, tiled=True),
    )
    product = lax.dot_general(
        spread_orbitals,
        spread_vectors,
        (((1,), (1,)), ((), ())),
        preferred_element_type=jnp.float32,
    )
    partial_rows = lax.psum_scatter(product * (1.0 / NPTS), "band", scatter_dimension=0, tiled=True)
    gram = lax.psum(partial_rows, "grid")
    return (vectors, gram)


def solution(mesh):
    return jax.shard_map(
        per_device,
        mesh=mesh,
        in_specs=(P("band", "grid", None), P()),
        out_specs=(P("band", "grid", None), P("band", None)),
        check_vma=False,
    )
```

profile of v0, /device:TPU:0, one launch (start us, length us, event | category | flops | bytes accessed | tf_op | source)
XLA Modules:
  0.0 1356.4 jit_solution(10697332559528059427)
XLA Ops:
  9.5 74.8 %all-reduce.3.cloned.1.call-done = bf16[16,4096]{1,0:T(8,128)(2,1)} async-done(((bf16[16,4096]{1,0:T(8,128)(2,1)}), bf16[16,4096]{1,0:T(8,128)(2,1)}) %all-reduce.3.cloned.1.call-update) | async-done | bytes 131088 | tf_op jit(solution)/shard_map/psum | solution.py:18
  97.4 27.0 %reshape.119 = f32[64,16,64,64]{3,2,1,0:T(8,128)} reshape(f32[64,16,4096]{2,1,0:T(8,128)} %convert_multiply_fusion) | data formatting | bytes 33554432 | tf_op jit(solution)/shard_map/reshape | solution.py:39
  124.4 33.2 %fusion.15 = f32[64,16,64,64]{3,2,1,0:T(8,128)} fusion(f32[64,16,64,64]{3,2,1,0:T(8,128)} %reshape.119), kind=kOutput, calls=%fused_computation.25 | convolution fusion | flops 3221286912 | bytes 33554432 | tf_op jit(solution)/shard_map/bxyz,zk->bxyk/dot_general | solution.py:40
  157.6 37.2 %convolution_bitcast_fusion.1 = f32[64,16,64,64]{3,2,1,0:T(8,128)} fusion(f32[64,16,64,64]{3,2,1,0:T(8,128)} %fusion.15), kind=kOutput, calls=%fused_computation.10 | convolution fusion | flops 3221286912 | bytes 33554432 | tf_op jit(solution)/shard_map/bxyz,yk->bxkz/dot_general | solution.py:41
  194.9 33.0 %copy.39 = f32[64,16,64,64]{0,1,3,2:T(8,128)} copy(f32[64,16,64,64]{3,2,1,0:T(8,128)} %convolution_bitcast_fusion.1) | data formatting | bytes 33554432 | tf_op jit(solution)/shard_map/reshape | solution.py:42
  227.9 42.5 %reshape.130 = f32[4,1,1048576]{2,1,0:T(1,128)} reshape(f32[4096,16,64]{2,1,0:T(8,128)} %bitcast.70) | data formatting | bytes 33554432
  278.0 182.4 %all-to-all-done = f32[4,1,1048576]{2,1,0:T(1,128)} async-done(((f32[4,1,1048576]{2,1,0:T(1,128)}), f32[4,1,1048576]{2,1,0:T(1,128)}, u32[]{:S(2)}, u32[]{:S(2)}) %all-to-all-start) | async-done | bytes 16777248 | tf_op jit(solution)/shard_map/all_to_all | solution.py:58
  461.0 54.2 %reduce = f32[4,1048576]{1,0:T(4,128)} reduce(f32[4,1,1048576]{2,1,0:T(1,128)} %all-to-all-done, f32[]{:T(128)} %broadcast.113), dimensions={1}, to_apply=%all_to_all.50.reduce_sub_computation | reduce | bytes 33554436 | tf_op jit(solution)/shard_map/all_to_all | solution.py:58
  515.2 55.1 %reshape.131 = f32[4096,16,64]{2,1,0:T(8,128)} reshape(f32[4,1048576]{1,0:T(4,128)} %reduce) | data formatting | bytes 33554432
  570.3 26.6 %copy.40 = f32[64,16,4,1024]{3,2,1,0:T(4,128)} copy(f32[64,16,4,1024]{0,1,3,2:T(8,128)} %bitcast.69) | data formatting | bytes 33554432 | tf_op jit(solution)/shard_map/all_to_all | solution.py:58
  596.9 20.4 %copy.28 = f32[64,4,16,1024]{3,2,1,0:T(8,128)} copy(f32[64,4,16,1024]{3,1,2,0:T(4,128)} %bitcast.71) | data formatting | bytes 33554432 | tf_op jit(solution)/shard_map/all_to_all | solution.py:58
  617.3 21.9 %fusion.20 = f32[64,64,1024]{2,0,1:T(8,128)} fusion(f32[64,64,1024]{2,1,0:T(8,128)} %bitcast.73), kind=kOutput, calls=%fused_computation.30 | convolution fusion | flops 3221286912 | bytes 33554432 | tf_op jit(solution)/shard_map/bxq,xk->bkq/dot_general | solution.py:56
  639.3 22.2 %fusion.5 = f32[64,64,1024]{2,1,0:T(8,128)} fusion(f32[64,64,1024]{2,0,1:T(8,128)} %fusion.20, f32[64,1024]{1,0:T(8,128)S(1)} %divide_select_fusion), kind=kOutput, calls=%fused_computation.11 | convolution fusion | flops 3225481216 | bytes 33816576 | tf_op jit(solution)/shard_map/bxq,xk->bkq/dot_general | solution.py:63
  710.7 158.8 %all-to-all-done.1 = f32[64,64,1024]{2,0,1:T(8,128)} async-done(((f32[64,64,1024]{2,0,1:T(8,128)}), f32[64,64,1024]{2,0,1:T(8,128)}, u32[]{:S(2)}, u32[]{:S(2)}) %all-to-all-start.1) | async-done | bytes 16777248 | tf_op jit(solution)/shard_map/all_to_all | solution.py:64
  874.6 20.9 %copy.50 = f32[64,4,16,1024]{3,1,2,0:T(4,128)} copy(f32[64,4,16,1024]{3,0,2,1:T(8,128)} %bitcast.14) | data formatting | bytes 33554432 | tf_op jit(solution)/shard_map/all_to_all | solution.py:64
  895.4 27.6 %reshape.121 = f32[64,16,64,64]{3,2,1,0:T(8,128)} reshape(f32[64,16,4,1024]{3,2,1,0:T(4,128)} %bitcast.72) | data formatting | bytes 33554432 | tf_op jit(solution)/shard_map/reshape | solution.py:39
  923.0 33.2 %fusion.13 = f32[64,16,64,64]{3,2,1,0:T(8,128)} fusion(f32[64,16,64,64]{3,2,1,0:T(8,128)} %reshape.121), kind=kOutput, calls=%fused_computation.23 | convolution fusion | flops 3221286912 | bytes 33554432 | tf_op jit(solution)/shard_map/bxyz,zk->bxyk/dot_general | solution.py:40
  956.3 37.3 %convolution_bitcast_fusion = f32[64,16,64,64]{3,2,1,0:T(8,128)} fusion(f32[64,16,64,64]{3,2,1,0:T(8,128)} %fusion.13), kind=kOutput, calls=%fused_computation.9 | convolution fusion | flops 3221286912 | bytes 33554432 | tf_op jit(solution)/shard_map/bxyz,yk->bxkz/dot_general | solution.py:41
  993.6 27.9 %reshape.123 = f32[64,8,8192]{2,1,0:T(8,128)} reshape(f32[64,16,64,64]{3,2,1,0:T(8,128)} %convolution_bitcast_fusion) | data formatting | bytes 33554432 | tf_op jit(solution)/shard_map/reshape | solution.py:42
  1039.1 18.5 %all-to-all-done.3 = bf16[64,8,8192]{2,0,1:T(8,128)(2,1)} async-done(((bf16[64,8,8192]{2,0,1:T(8,128)(2,1)}), bf16[64,8,8192]{2,0,1:T(8,128)(2,1)}, u32[]{:S(2)}, u32[]{:S(2)}) %all-to-all-start.3) | async-done | bytes 8388640 | tf_op jit(solution)/shard_map/all_to_all | solution.py:87
  1057.6 186.9 %all_to_all.68 = bf16[64,8,8192]{2,0,1:T(8,128)(2,1)S(1)} all-to-all(bf16[64,8,8192]{2,0,1:T(8,128)(2,1)} %fusion.3), channel_id=1, replica_groups=mesh['band'=8,'grid'=4] {'band'}, dimensions={1} | all-to-all | bytes 16777216 | tf_op jit(solution)/shard_map/all_to_all | solution.py:88
  1252.9 28.0 %reshape.122 = f32[64,16,4096]{2,1,0:T(8,128)} reshape(f32[64,16,64,64]{3,2,1,0:T(8,128)} %convolution_bitcast_fusion) | data formatting | bytes 33554432 | tf_op jit(solution)/shard_map/reshape | solution.py:42
  1281.0 33.7 %reduce-scatter.4.cloned.1.call-done = f32[64,512]{1,0:T(8,128)} async-done(((f32[512,512]{1,0:T(8,128)}), f32[64,512]{1,0:T(8,128)}) %reduce-scatter.4.cloned.1.call-update) | async-done | bytes 131088
  1325.9 22.1 %all-reduce.5.cloned.1.call-done = f32[64,512]{0,1:T(8,128)} async-done(((f32[64,512]{0,1:T(8,128)}), f32[64,512]{0,1:T(8,128)}) %all-reduce.5.cloned.1.call-update) | async-done | bytes 131088 | tf_op jit(solution)/shard_map/psum | solution.py:97
  (37 shorter events, 116.1 us)
Async XLA Ops:
  7.2 77.1 %all-reduce.3.cloned.1.call-start = ((), (), s32[]{:S(2)}) async-start(), calls=%async_computation.5 | async-start | bytes 262144 | tf_op jit(solution)/shard_map/psum | solution.py:18
  85.2 0.7 copy-start
  270.4 190.0 %all-to-all-start = ((f32[4,1,1048576]{2,1,0:T(1,128)}), f32[4,1,1048576]{2,1,0:T(1,128)}, u32[]{:S(2)}, u32[]{:S(2)}) async-start(f32[4,1,1048576]{2,1,0:T(1,128)} %reshape.130), calls=%async_computation | async-start | bytes 33554432 | tf_op jit(solution)/shard_map/all_to_all | solution.py:58
  679.2 190.2 %all-to-all-start.1 = ((f32[64,64,1024]{2,0,1:T(8,128)}), f32[64,64,1024]{2,0,1:T(8,128)}, u32[]{:S(2)}, u32[]{:S(2)}) async-start(f32[64,64,1024]{2,0,1:T(8,128)} %copy.29), calls=%async_computation.1 | async-start | bytes 33554432 | tf_op jit(solution)/shard_map/all_to_all | solution.py:64
  699.4 175.1 %copy-start.2 = (bf16[16,4096]{1,0:T(8,128)(2,1)S(1)}, bf16[16,4096]{1,0:T(8,128)(2,1)}, u32[]{:S(2)}) copy-start(bf16[16,4096]{1,0:T(8,128)(2,1)} %all-reduce.3.cloned.1.call-done) | copy-start | bytes 393220
  869.4 188.2 %all-to-all-start.3 = ((bf16[64,8,8192]{2,0,1:T(8,128)(2,1)}), bf16[64,8,8192]{2,0,1:T(8,128)(2,1)}, u32[]{:S(2)}, u32[]{:S(2)}) async-start(bf16[64,8,8192]{2,0,1:T(8,128)(2,1)} %copy.33), calls=%async_computation.3 | async-start | bytes 16777216 | tf_op jit(solution)/shard_map/all_to_all | solution.py:87
  874.5 440.2 %reduce-scatter.4.cloned.1.call-start = ((), (), s32[]{:S(2)}) async-start(), calls=%async_computation.7 | async-start | bytes 1179648
  1252.9 63.5 %copy-start.1 = (f32[16,4096]{1,0:T(8,128)S(1)}, f32[16,4096]{1,0:T(8,128)}, u32[]{:S(2)}) copy-start(f32[16,4096]{1,0:T(8,128)} %copy-done) | copy-start | bytes 786436
  1252.9 95.1 %all-reduce.5.cloned.1.call-start = ((), (), s32[]{:S(2)}) async-start(), calls=%async_computation.6 | async-start | bytes 524288 | tf_op jit(solution)/shard_map/psum | solution.py:97
Sparse Core Ops, SparseCore 0:
  11.9 72.3 all-reduce.2
  1253.0 61.5 reduce-scatter.3
  1317.0 30.9 all-reduce.4
where the time goes:
time: 1370 us; the launch traced here: 1360 us
  waiting for transfers between devices  490 us (36%)
  local copies, waits for them, and re-layouts  358 us (26%)
  matrix products  192 us (14%)
  blocking collectives  187 us (14%)
  other arithmetic  95.4 us (7%)
  starting transfers between devices  19.3 us (1%)
  between operations  14.7 us (1%)
    all_to_all x1, blocking collectives, per_device(): lax.all_to_all(flat_vectors, 'band', split_axis=1, concat_axis=0, tiled=T...  187 us
    all_to_all x1, waiting for transfers between devices, solve_potential(): lax.all_to_all(spectral, 'grid', split_axis=2, concat_axis=1, tiled=True)  182 us
    all_to_all x1, waiting for transfers between devices, solve_potential(): lax.all_to_all(moved, 'grid', split_axis=1, concat_axis=2, tiled=True)  159 us
    unnamed x11, local copies, waits for them, and re-layouts  103 us
    reshape x3, local copies, waits for them, and re-layouts, transform_planes(): return shaped.reshape(batch, planes, square)  89 us
    psum x1, waiting for transfers between devices, spread(): return lax.psum(kept, axis)  74.8 us
    dot_general x2, matrix products, transform_planes(): shaped = jnp.einsum('bxyz,yk->bxkz', shaped, matrix, precision=HIGHEST)  74.5 us
    dot_general x2, matrix products, transform_planes(): shaped = jnp.einsum('bxyz,zk->bxyk', shaped, matrix, precision=HIGHEST)  66.5 us
  transfers between devices with their start and end apart: 6, of which 6 were waited for; matrix products, arithmetic and copies ran while one was open for 16% of the time, Pallas kernels for 0%

commit v1 on v0

v1 whole, which is shorter than its diff:
```python
import math

import jax
import jax.numpy as jnp
from jax import lax
from jax.experimental import pallas as pl
from jax.experimental.pallas import tpu as pltpu
from jax.sharding import PartitionSpec as P

NG = 64
NPTS = 262144
KERNEL_SCALE = 128.0
BF = jnp.bfloat16
F32 = jnp.float32


def spread(value, axis, source):
    kept = jnp.where(lax.axis_index(axis) == source, value, 0).astype(value.dtype)
    return lax.psum(kept, axis)


def cas_matrix(length):
    products = (
        jnp.arange(length, dtype=jnp.int32)[:, None]
        * jnp.arange(length, dtype=jnp.int32)[None, :]
        % length
    )
    angles = products.astype(F32) * (2.0 * math.pi / length)
    return jnp.cos(angles) + jnp.sin(angles)


def halves(value):
    high = value.astype(BF)
    return high, (value - high.astype(F32)).astype(BF)


def matrix_halves(value):
    high = lax.reduce_precision(value, 8, 7)
    return high.astype(BF), (value - high).astype(BF)


def kernel_table():
    frequency = jnp.arange(NG, dtype=jnp.int32)
    folded = jnp.minimum(frequency, NG - frequency).astype(F32)
    square = folded * folded
    summed = square[:, None, None] + square[None, :, None] + square[None, None, :]
    table = jnp.where(summed > 0, KERNEL_SCALE / NPTS / jnp.maximum(summed, 1.0), 0.0)
    return jnp.concatenate([table, table], axis=2)


def dot(a, b):
    return jnp.dot(a, b, preferred_element_type=F32)


def solve_body(slabs, rows, orb, partner, table, left_hi, left_lo, right_hi, right_lo, out, work):
    def along_rows(value):
        high, low = halves(value)
        both = dot(left_hi[...], jnp.concatenate([high, low], axis=1))
        return both[:, :128] + both[:, 128:] + dot(left_lo[...], high)

    def along_lanes(value):
        high, low = halves(value)
        return dot(jnp.concatenate([high, low], axis=1), right_hi[...]) + dot(high, right_lo[...])

    for slab in range(slabs):
        @pl.loop(0, rows // 4, unroll=2)
        def _(i):
            at = pl.ds(i * 4, 4)
            x = slab * rows + i * 4
            field = orb[slab, 0, at].astype(F32) * partner[pl.ds(x, 4)].astype(F32)
            field = along_rows(along_lanes(field.reshape(256, 128)))
            work[pl.ds(x, 4)] = field.reshape(4, NG, 128)

    @pl.loop(0, NG // 8)
    def _(i):
        at = pl.ds(pl.multiple_of(i * 8, 8), 8)
        planes = jnp.swapaxes(work[:, at, :], 0, 1)
        done = []
        for part in range(2):
            field = planes[part * 4:part * 4 + 4].reshape(256, 128)
            field = along_rows(field) * table[pl.ds(i * 8 + part * 4, 4)].reshape(256, 128)
            done.append(along_rows(field).reshape(4, NG, 128))
        work[:, at, :] = jnp.swapaxes(jnp.concatenate(done, axis=0), 0, 1)

    for slab in range(slabs):
        @pl.loop(0, rows // 4, unroll=2)
        def _(i):
            x = slab * rows + i * 4
            field = along_lanes(along_rows(work[pl.ds(x, 4)].reshape(256, 128)))
            field = field.reshape(4, NG, 128) * partner[pl.ds(x, 4)].astype(F32)
            out[slab, 0, pl.ds(i * 4, 4)] = (-field).astype(BF)


def solve(pairs, partner):
    slabs, count, rows = pairs.shape[:3]
    matrix = cas_matrix(NG)
    left = matrix_halves(jnp.kron(jnp.eye(4, dtype=F32), matrix))
    right = matrix_halves(jnp.kron(jnp.eye(2, dtype=F32), matrix))
    right_hi = jnp.concatenate([right[0], right[0]], axis=0)
    block = pl.BlockSpec((slabs, 1, rows, NG, 128), lambda i: (0, i, 0, 0, 0))
    whole = lambda array: pl.BlockSpec(array.shape, lambda i: (0,) * array.ndim)
    fixed = (partner, kernel_table(), left[0], left[1], right_hi, right[1])
    return pl.pallas_call(
        lambda *refs: solve_body(slabs, rows, *refs),
        grid=(count,),
        in_specs=[block] + [whole(a) for a in fixed],
        out_specs=block,
        out_shape=jax.ShapeDtypeStruct(pairs.shape, BF),
        scratch_shapes=[pltpu.VMEM((NG, NG, 128), F32)],
        compiler_params=pltpu.CompilerParams(vmem_limit_bytes=48 * 1024 * 1024),
        cost_estimate=pl.CostEstimate(
            flops=count * 60 * NG * NG * 128 * 256, bytes_accessed=4 * pairs.size, transcendentals=0
        ),
    )(pairs, *fixed)


def gram_body(left, right, out):
    @pl.when(pl.program_id(0) == 0)
    def _():
        out[...] = jnp.zeros_like(out)

    size = out.shape[0]
    a = left[:, 0].reshape(size, left.shape[3])
    b = right[:, 0].reshape(size, right.shape[3])
    out[...] += lax.dot_general(a, b, (((1,), (1,)), ((), ())), preferred_element_type=F32)


def gram_product(left, right):
    shares, planes, bands, points = left.shape
    size = shares * bands
    if bands % 16 or points % 128:
        return jnp.einsum("gxbk,hxck->gbhc", left, right, preferred_element_type=F32).reshape(size, size)
    block = pl.BlockSpec((shares, 1, bands, points), lambda i: (0, i, 0, 0))
    return pl.pallas_call(
        gram_body,
        grid=(planes,),
        in_specs=[block, block],
        out_specs=pl.BlockSpec((size, size), lambda i: (0, 0)),
        out_shape=jax.ShapeDtypeStruct((size, size), F32),
        compiler_params=pltpu.CompilerParams(vmem_limit_bytes=32 * 1024 * 1024),
        cost_estimate=pl.CostEstimate(
            flops=2 * size * size * planes * points, bytes_accessed=4 * left.size, transcendentals=0
        ),
    )(left, right)


def to_shares(array):
    shares = lax.axis_size("band")
    bands, planes, square = array.shape
    cut = array.reshape(bands, planes, shares, square // shares).transpose(2, 1, 0, 3)
    return lax.all_to_all(cut, "band", split_axis=0, concat_axis=0)


def per_device(orbitals, picks):
    bands, planes, square = orbitals.shape
    groups = lax.axis_size("grid")
    pairs = bands // groups // 2
    target = picks[0]
    mine = lax.dynamic_index_in_dim(orbitals, target % bands, 0, keepdims=False)
    slab = spread(mine, "band", target // bands).reshape(planes, NG, NG)
    partner = lax.all_gather(jnp.concatenate([slab, slab], axis=2), "grid", axis=0, tiled=True)

    paired = orbitals.reshape(groups, pairs, 2, planes, NG, NG).transpose(0, 1, 3, 4, 2, 5)
    paired = paired.reshape(groups, pairs, planes, NG, 128)
    cubes = lax.all_to_all(paired, "grid", split_axis=0, concat_axis=0)
    spread_orbitals = to_shares(orbitals)
    solved = solve(cubes, partner)
    back = lax.all_to_all(solved, "grid", split_axis=0, concat_axis=0)
    vectors = back.reshape(groups, pairs, planes, NG, 2, NG).transpose(0, 1, 4, 2, 3, 5)
    vectors = vectors.reshape(bands, planes, square)
    spread_vectors = to_shares(vectors)
    product = gram_product(spread_orbitals, spread_vectors)
    partial_rows = lax.psum_scatter(product * (1.0 / NPTS), "band", scatter_dimension=0, tiled=True)
    gram = lax.psum(partial_rows, "grid")
    return (vectors, gram)


def solution(mesh):
    return jax.shard_map(
        per_device,
        mesh=mesh,
        in_specs=(P("band", "grid", None), P()),
        out_specs=(P("band", "grid", None), P("band", None)),
        check_vma=False,
    )
```

time: 1370 us -> 933 us (0.68)
  matrix products: 192 us -> 0 us
  Pallas kernels: 0 us -> 155 us
  local copies, waits for them, and re-layouts: 358 us -> 208 us
  waiting for transfers between devices: 490 us -> 341 us
  other arithmetic: 95.4 us -> 5.65 us
    dot_general x7 -> x0, matrix products: 192 us -> none  [the longest x2 74.5 us: transform_planes(): shaped = jnp.einsum('bxyz,yk->bxkz', shaped, matrix, precision=HIGHEST)]
    all_to_all x3, waiting for transfers between devices: 360 us -> 175 us  [the longest x1 106 us: to_shares(): return lax.all_to_all(cut, 'band', split_axis=0, concat_axis=0)]
    pallas_call x0 -> x2, Pallas kernels: none -> 155 us  [the longest x1 142 us: solve(): pl.pallas_call(lambda *refs: solve_body(slabs, rows, *refs), grid=(count,...]
    all_to_all x6 -> x0, local copies, waits for them, and re-layouts: 92.7 us -> none  [the longest x3 47.5 us: solve_potential(): lax.all_to_all(spectral, 'grid', split_axis=2, concat_axis=1, tiled=True)]
    unnamed x11 -> x4, local copies, waits for them, and re-layouts: 103 us -> 15 us
    reduce_scatter x0 -> x1, waiting for transfers between devices: none -> 61.6 us  [per_device(): lax.psum_scatter(product * (1.0 / NPTS), 'band', scatter_dimension=0, til...]
    all_to_all x1 -> x0, other arithmetic: 54.2 us -> none  [solve_potential(): lax.all_to_all(spectral, 'grid', split_axis=2, concat_axis=1, tiled=True)]
    another operation x0 -> x2, local copies, waits for them, and re-layouts: none -> 33.8 us  [to_shares(): array.reshape(bands, planes, shares, square // shares).transpose(2, 1, 0, 3)]
  transfers between devices with their start and end apart: 6 -> 7, of which waited for: 6 -> 6; matrix products, arithmetic and copies ran while one was open for 16% -> 14% of each run, Pallas kernels for 0% -> 0%
where the time goes in v1:
time: 933 us; the launch traced here: 929 us
  waiting for transfers between devices  341 us (37%)
  local copies, waits for them, and re-layouts  208 us (22%)
  blocking collectives  187 us (20%)
  Pallas kernels  155 us (17%)
  starting transfers between devices  18.2 us (2%)
  between operations  14.5 us (2%)
    all_to_all x1, blocking collectives, to_shares(): return lax.all_to_all(cut, 'band', split_axis=0, concat_axis=0)  187 us
    pallas_call x1, Pallas kernels, solve(): pl.pallas_call(lambda *refs: solve_body(slabs, rows, *refs), grid=(count,...  142 us
    all_to_all x1, waiting for transfers between devices, to_shares(): return lax.all_to_all(cut, 'band', split_axis=0, concat_axis=0)  106 us
    psum x1, waiting for transfers between devices, spread(): return lax.psum(kept, axis)  74.6 us
    all_to_all x1, waiting for transfers between devices, per_device(): back = lax.all_to_all(solved, 'grid', split_axis=0, concat_axis=0)  69.4 us
    reduce_scatter x1, waiting for transfers between devices, per_device(): lax.psum_scatter(product * (1.0 / NPTS), 'band', scatter_dimension=0, til...  61.6 us
    reshape x2, local copies, waits for them, and re-layouts, per_device(): orbitals.reshape(groups, pairs, 2, planes, NG, NG)  54.4 us
    reshape x2, local copies, waits for them, and re-layouts, per_device(): back.reshape(groups, pairs, planes, NG, 2, NG).transpose(0, 1, 4, 2, 3, 5)  43 us
  transfers between devices with their start and end apart: 7, of which 6 were waited for; matrix products, arithmetic and copies ran while one was open for 14% of the time, Pallas kernels for 0%

profile of v1, /device:TPU:0, one launch (start us, length us, event | category | flops | bytes accessed | tf_op | source)
XLA Modules:
  0.0 929.2 jit_solution(14104385010902799118)
XLA Ops:
  7.2 23.6 %reshape.135 = bf16[4,8,2,16,64,64]{5,4,3,2,1,0:T(8,128)(2,1)} reshape(bf16[64,16,4096]{2,1,0:T(8,128)(2,1)} %param.2) | data formatting | bytes 16777216 | tf_op jit(solution)/shard_map/reshape | solution.py:163
  30.7 30.8 %copy.20 = bf16[4,8,2,16,64,64]{5,2,4,3,1,0:T(2,128)(2,1)} copy(bf16[4,8,2,16,64,64]{5,4,3,2,1,0:T(8,128)(2,1)} %reshape.135) | data formatting | bytes 16777216 | tf_op jit(solution)/shard_map/reshape | solution.py:163
  61.6 26.9 %reshape.136 = bf16[4,8,16,64,128]{4,3,2,1,0:T(8,128)(2,1)} reshape(bf16[4,8,16,64,2,64]{5,4,3,2,1,0:T(2,128)(2,1)} %bitcast.29) | data formatting | bytes 16777216 | tf_op jit(solution)/shard_map/reshape | solution.py:164
  88.5 5.6 all-to-all-start
  97.5 74.6 %all-reduce.3.cloned.1.call-done = bf16[16,64,64]{2,1,0:T(8,128)(2,1)} async-done(((bf16[16,64,64]{2,1,0:T(8,128)(2,1)}), bf16[16,64,64]{2,1,0:T(8,128)(2,1)}) %all-reduce.3.cloned.1.call-update) | async-done | bytes 131088 | tf_op jit(solution)/shard_map/psum | solution.py:19
  172.1 1.9 pad_maximum_fusion.1
  175.7 19.2 %all-gather.2.cloned.1.call-done.refs_1_ = bf16[64,64,128]{2,1,0:T(8,128)(2,1)} async-done(((bf16[16,64,128]{2,1,0:T(8,128)(2,1)}), bf16[64,64,128]{2,1,0:T(8,128)(2,1)}) %all-gather.2.cloned.1.call-update) | async-done | bytes 1048592 | tf_op jit(solution)/shard_map/all_gather | solution.py:161
  196.1 141.5 %shard_map.41 = bf16[4,8,16,64,128]{4,3,2,1,0:T(8,128)(2,1)} custom-call(bf16[4,8,16,64,128]{4,3,2,1,0:T(8,128)(2,1)} %all-to-all-done.refs_0_, bf16[64,64,128]{2,1,0:T(8,128)(2,1)S(1)} %copy-done, f32[64,64,128]{2,1,0:T(8,128)S(1)} %pad_maximum_fusion.refs_2_, bf16[256,256]{1,0:T(8,128)(2,1)S(1)} %get-tuple-element.3.refs_3_, ...), custom_call_target="tpu_custom_call" | custom-call | flops 64424509440 | bytes 16777216 | tf_op jit(solution)/shard_map/pallas_call | solution.py:103
  337.7 5.8 all-to-all-start.1
  343.5 12.2 %copy.14 = bf16[128,8,8,512]{3,2,1,0:T(8,128)(2,1)} copy(bf16[128,8,8,512]{3,1,2,0:T(8,128)(2,1)} %bitcast.30) | data formatting | bytes 16777216
  355.7 11.3 %copy.22 = bf16[64,16,8,512]{3,0,1,2:T(8,128)(2,1)} copy(bf16[64,16,8,512]{3,2,1,0:T(8,128)(2,1)} %bitcast.33) | data formatting | bytes 16777216 | tf_op jit(solution)/shard_map/reshape | solution.py:150
  367.0 69.4 %all-to-all-done.1 = bf16[4,8,16,64,128]{4,3,2,1,0:T(8,128)(2,1)} async-done(((bf16[4,8,16,64,128]{4,3,2,1,0:T(8,128)(2,1)}), bf16[4,8,16,64,128]{4,3,2,1,0:T(8,128)(2,1)}, u32[]{:S(2)}, u32[]{:S(2)}) %all-to-all-start.1) | async-done | bytes 8388640 | tf_op jit(solution)/shard_map/all_to_all | solution.py:168
  436.5 6.4 all-to-all-start.2
  443.1 27.8 %reshape.138 = bf16[4,8,16,64,2,64]{5,4,3,2,1,0:T(2,128)(2,1)} reshape(bf16[4,8,16,64,128]{4,3,2,1,0:T(8,128)(2,1)} %all-to-all-done.1) | data formatting | bytes 16777216 | tf_op jit(solution)/shard_map/reshape | solution.py:169
  471.0 15.1 %copy.19 = bf16[4,8,16,64,2,64]{5,3,2,4,1,0:T(8,128)(2,1)} copy(bf16[4,8,16,64,2,64]{5,4,3,2,1,0:T(2,128)(2,1)} %reshape.138) | data formatting | bytes 16777216 | tf_op jit(solution)/shard_map/reshape | solution.py:169
  486.1 22.4 %reshape_reshape.3 = bf16[64,16,8,512]{3,2,1,0:T(8,128)(2,1)} reshape(bf16[4,8,2,16,64,64]{5,4,3,2,1,0:T(8,128)(2,1)} %bitcast.27) | data formatting | bytes 16777216 | tf_op jit(solution)/shard_map/reshape;reshape | solution.py:150
  508.6 11.3 %copy.21 = bf16[64,16,8,512]{3,0,1,2:T(8,128)(2,1)} copy(bf16[64,16,8,512]{3,2,1,0:T(8,128)(2,1)} %reshape_reshape.3) | data formatting | bytes 16777216 | tf_op jit(solution)/shard_map/reshape;reshape | solution.py:150
  519.9 105.9 %all-to-all-done.2.left = bf16[8,16,64,512]{3,2,1,0:T(8,128)(2,1)} async-done(((bf16[8,16,64,512]{3,2,1,0:T(8,128)(2,1)}), bf16[8,16,64,512]{3,2,1,0:T(8,128)(2,1)}, u32[]{:S(2)}, u32[]{:S(2)}) %all-to-all-start.2) | async-done | bytes 8388640 | tf_op jit(solution)/shard_map/all_to_all | solution.py:151
  625.9 186.9 %all_to_all.20.right = bf16[8,16,64,512]{3,2,1,0:T(8,128)(2,1)S(1)} all-to-all(bf16[8,16,64,512]{3,2,1,0:T(8,128)(2,1)} %bitcast.32), channel_id=1, replica_groups=mesh['band'=8,'grid'=4] {'band'}, dimensions={0} | all-to-all | bytes 16777216 | tf_op jit(solution)/shard_map/all_to_all | solution.py:151
  812.7 13.1 %shard_map.42 = f32[512,512]{1,0:T(8,128)S(1)} custom-call(bf16[8,16,64,512]{3,2,1,0:T(8,128)(2,1)} %all-to-all-done.2.left, bf16[8,16,64,512]{3,2,1,0:T(8,128)(2,1)S(1)} %all_to_all.20.right), custom_call_target="tpu_custom_call" | custom-call | flops 4294967296 | bytes 16777216 | tf_op jit(solution)/shard_map/pallas_call | solution.py:134
  826.9 61.6 %reduce-scatter.2.cloned.1.call-done = f32[64,512]{1,0:T(8,128)} async-done(((f32[512,512]{1,0:T(8,128)}), f32[64,512]{1,0:T(8,128)}) %reduce-scatter.2.cloned.1.call-update) | async-done | bytes 131088 | tf_op jit(solution)/shard_map/reduce_scatter | solution.py:173
  888.5 22.6 %reshape.139 = bf16[64,16,4096]{2,1,0:T(8,128)(2,1)} reshape(bf16[4,8,2,16,64,64]{5,4,3,2,1,0:T(8,128)(2,1)} %bitcast.28) | data formatting | bytes 16777216 | tf_op jit(solution)/shard_map/reshape | solution.py:170
  911.1 10.0 %all-reduce.5.cloned.1.call-done = f32[64,512]{1,0:T(8,128)} async-done(((f32[64,512]{1,0:T(8,128)}), f32[64,512]{1,0:T(8,128)}) %all-reduce.5.cloned.1.call-update) | async-done | bytes 131088 | tf_op jit(solution)/shard_map/psum | solution.py:174
  921.1 1.6 copy.26
  (28 shorter events, 6.9 us)
Async XLA Ops:
  88.5 106.4 %all-to-all-start = ((bf16[4,8,16,64,128]{4,3,2,1,0:T(8,128)(2,1)}), bf16[4,8,16,64,128]{4,3,2,1,0:T(8,128)(2,1)}, u32[]{:S(2)}, u32[]{:S(2)}) async-start(bf16[4,8,16,64,128]{4,3,2,1,0:T(8,128)(2,1)} %reshape.136), calls=%async_computation | async-start | bytes 16777216 | tf_op jit(solution)/shard_map/all_to_all | solution.py:165
  94.1 78.0 %all-reduce.3.cloned.1.call-start = ((), (), s32[]{:S(2)}) async-start(), calls=%async_computation.5 | async-start | bytes 524288 | tf_op jit(solution)/shard_map/psum | solution.py:19
  96.8 98.1 %all-gather.2.cloned.1.call-start = ((), (), s32[]{:S(2)}) async-start(), calls=%async_computation.6 | async-start | bytes 1310720 | tf_op jit(solution)/shard_map/all_gather | solution.py:161
  194.9 1.2 copy-start
  337.7 98.8 %all-to-all-start.1 = ((bf16[4,8,16,64,128]{4,3,2,1,0:T(8,128)(2,1)}), bf16[4,8,16,64,128]{4,3,2,1,0:T(8,128)(2,1)}, u32[]{:S(2)}, u32[]{:S(2)}) async-start(bf16[4,8,16,64,128]{4,3,2,1,0:T(8,128)(2,1)} %shard_map.41), calls=%async_computation.1 | async-start | bytes 16777216 | tf_op jit(solution)/shard_map/all_to_all | solution.py:168
  436.5 189.4 %all-to-all-start.2 = ((bf16[8,16,64,512]{3,2,1,0:T(8,128)(2,1)}), bf16[8,16,64,512]{3,2,1,0:T(8,128)(2,1)}, u32[]{:S(2)}, u32[]{:S(2)}) async-start(bf16[8,16,64,512]{3,2,1,0:T(8,128)(2,1)} %bitcast.31), calls=%async_computation.2 | async-start | bytes 16777216 | tf_op jit(solution)/shard_map/all_to_all | solution.py:151
  442.9 445.6 %reduce-scatter.2.cloned.1.call-start = ((), (), s32[]{:S(2)}) async-start(), calls=%async_computation.7 | async-start | bytes 1179648 | tf_op jit(solution)/shard_map/reduce_scatter | solution.py:173
  826.9 94.2 %all-reduce.5.cloned.1.call-start = ((), (), s32[]{:S(2)}) async-start(), calls=%async_computation.8 | async-start | bytes 262144 | tf_op jit(solution)/shard_map/psum | solution.py:174
Sparse Core Ops, SparseCore 0:
  98.3 73.7 all-reduce.2
  174.2 20.7 all-gather.1
  827.0 61.4 reduce-scatter.1
  890.7 30.4 all-reduce.4

commit v2 on v1

--- a/solution.py
+++ b/solution.py
@@ -165,6 +165,7 @@
     cubes = lax.all_to_all(paired, "grid", split_axis=0, concat_axis=0)
     spread_orbitals = to_shares(orbitals)
     solved = solve(cubes, partner)
+    solved, spread_orbitals = lax.optimization_barrier((solved, spread_orbitals))
     back = lax.all_to_all(solved, "grid", split_axis=0, concat_axis=0)
     vectors = back.reshape(groups, pairs, planes, NG, 2, NG).transpose(0, 1, 4, 2, 3, 5)
     vectors = vectors.reshape(bands, planes, square)

time: 933 us -> 1060 us (1.14)
  blocking collectives: 187 us -> 289 us
  waiting for transfers between devices: 341 us -> 375 us
    psum x1, waiting for transfers between devices: 74.6 us -> 219 us  [spread(): return lax.psum(kept, axis)]
    all_to_all x1, waiting for transfers between devices: 106 us -> 0.01 us  [to_shares(): return lax.all_to_all(cut, 'band', split_axis=0, concat_axis=0)]
    all_to_all x0 -> x1, blocking collectives: none -> 101 us  [per_device(): back = lax.all_to_all(solved, 'grid', split_axis=0, concat_axis=0)]
    all_to_all x1, waiting for transfers between devices: 0.01 us -> 70.2 us  [per_device(): cubes = lax.all_to_all(paired, 'grid', split_axis=0, concat_axis=0)]
    all_to_all x1 -> x0, waiting for transfers between devices: 69.4 us -> none  [per_device(): back = lax.all_to_all(solved, 'grid', split_axis=0, concat_axis=0)]
  transfers between devices with their start and end apart: 7 -> 6, of which waited for: 6 -> 5; matrix products, arithmetic and copies ran while one was open for 14% -> 5% of each run, Pallas kernels for 0% -> 13%
where the time goes in v2:
time: 1060 us
  waiting for transfers between devices  375 us (35%)
  blocking collectives  289 us (27%)
  local copies, waits for them, and re-layouts  208 us (20%)
  Pallas kernels  155 us (15%)
  between operations  14.5 us (1%)
  starting transfers between devices  12.7 us (1%)
    psum x1, waiting for transfers between devices, spread(): return lax.psum(kept, axis)  219 us
    all_to_all x1, blocking collectives, to_shares(): return lax.all_to_all(cut, 'band', split_axis=0, concat_axis=0)  189 us
    pallas_call x1, Pallas kernels, solve(): pl.pallas_call(lambda *refs: solve_body(slabs, rows, *refs), grid=(count,...  142 us
    all_to_all x1, blocking collectives, per_device(): back = lax.all_to_all(solved, 'grid', split_axis=0, concat_axis=0)  101 us
    all_to_all x1, waiting for transfers between devices, per_device(): cubes = lax.all_to_all(paired, 'grid', split_axis=0, concat_axis=0)  70.2 us
    reduce_scatter x1, waiting for transfers between devices, per_device(): lax.psum_scatter(product * (1.0 / NPTS), 'band', scatter_dimension=0, til...  61.1 us
    reshape x2, local copies, waits for them, and re-layouts, per_device(): orbitals.reshape(groups, pairs, 2, planes, NG, NG)  54.4 us
    reshape x2, local copies, waits for them, and re-layouts, per_device(): back.reshape(groups, pairs, planes, NG, 2, NG).transpose(0, 1, 4, 2, 3, 5)  43 us
  transfers between devices with their start and end apart: 6, of which 5 were waited for; matrix products, arithmetic and copies ran while one was open for 5% of the time, Pallas kernels for 13%

profile of v2, /device:TPU:0, one launch (start us, length us, event | category | flops | bytes accessed | tf_op | source)
XLA Modules:
  0.0 1060.6 jit_solution(15506277433767841865)
XLA Ops:
  7.2 23.6 %reshape.135 = bf16[4,8,2,16,64,64]{5,4,3,2,1,0:T(8,128)(2,1)} reshape(bf16[64,16,4096]{2,1,0:T(8,128)(2,1)} %param.2) | data formatting | bytes 16777216 | tf_op jit(solution)/shard_map/reshape | solution.py:163
  30.7 30.8 %copy.20 = bf16[4,8,2,16,64,64]{5,2,4,3,1,0:T(2,128)(2,1)} copy(bf16[4,8,2,16,64,64]{5,4,3,2,1,0:T(8,128)(2,1)} %reshape.135) | data formatting | bytes 16777216 | tf_op jit(solution)/shard_map/reshape | solution.py:163
  61.6 26.9 %reshape.136 = bf16[4,8,16,64,128]{4,3,2,1,0:T(8,128)(2,1)} reshape(bf16[4,8,16,64,2,64]{5,4,3,2,1,0:T(2,128)(2,1)} %bitcast.29) | data formatting | bytes 16777216 | tf_op jit(solution)/shard_map/reshape | solution.py:164
  88.5 5.8 all-to-all-start
  94.3 12.2 %copy.14 = bf16[128,8,8,512]{3,2,1,0:T(8,128)(2,1)} copy(bf16[128,8,8,512]{3,1,2,0:T(8,128)(2,1)} %bitcast.30) | data formatting | bytes 16777216
  106.5 11.4 %copy.22 = bf16[64,16,8,512]{3,0,1,2:T(8,128)(2,1)} copy(bf16[64,16,8,512]{3,2,1,0:T(8,128)(2,1)} %bitcast.33) | data formatting | bytes 16777216 | tf_op jit(solution)/shard_map/reshape | solution.py:150
  117.9 70.2 %all-to-all-done.refs_0_ = bf16[4,8,16,64,128]{4,3,2,1,0:T(8,128)(2,1)} async-done(((bf16[4,8,16,64,128]{4,3,2,1,0:T(8,128)(2,1)}), bf16[4,8,16,64,128]{4,3,2,1,0:T(8,128)(2,1)}, u32[]{:S(2)}, u32[]{:S(2)}) %all-to-all-start) | async-done | bytes 8388640 | tf_op jit(solution)/shard_map/all_to_all | solution.py:165
  188.1 6.5 all-to-all-start.1
  198.2 219.3 %all-reduce.3.cloned.1.call-done = bf16[16,64,64]{2,1,0:T(8,128)(2,1)} async-done(((bf16[16,64,64]{2,1,0:T(8,128)(2,1)}), bf16[16,64,64]{2,1,0:T(8,128)(2,1)}) %all-reduce.3.cloned.1.call-update) | async-done | bytes 131088 | tf_op jit(solution)/shard_map/psum | solution.py:19
  417.5 1.9 pad_maximum_fusion.1
  421.1 14.7 %all-gather.2.cloned.1.call-done.refs_1_ = bf16[64,64,128]{2,1,0:T(8,128)(2,1)} async-done(((bf16[16,64,128]{2,1,0:T(8,128)(2,1)}), bf16[64,64,128]{2,1,0:T(8,128)(2,1)}) %all-gather.2.cloned.1.call-update) | async-done | bytes 1048592 | tf_op jit(solution)/shard_map/all_gather | solution.py:161
  435.7 1.2 copy-done
  437.0 141.5 %shard_map.41 = bf16[4,8,16,64,128]{4,3,2,1,0:T(8,128)(2,1)} custom-call(bf16[4,8,16,64,128]{4,3,2,1,0:T(8,128)(2,1)} %all-to-all-done.refs_0_, bf16[64,64,128]{2,1,0:T(8,128)(2,1)S(1)} %copy-done, f32[64,64,128]{2,1,0:T(8,128)S(1)} %pad_maximum_fusion.refs_2_, bf16[256,256]{1,0:T(8,128)(2,1)S(1)} %get-tuple-element.7.refs_3_, ...), custom_call_target="tpu_custom_call" | custom-call | flops 64424509440 | bytes 16777216 | tf_op jit(solution)/shard_map/pallas_call | solution.py:103
  578.5 100.6 %all_to_all.20 = bf16[4,8,16,64,128]{4,3,2,1,0:T(8,128)(2,1)} all-to-all(bf16[4,8,16,64,128]{4,3,2,1,0:T(8,128)(2,1)} %shard_map.41), channel_id=1, replica_groups=mesh['band'=8,'grid'=4] {'grid'}, dimensions={0} | all-to-all | bytes 16777216 | tf_op jit(solution)/shard_map/all_to_all | solution.py:169
  679.1 27.8 %reshape.139 = bf16[4,8,16,64,2,64]{5,4,3,2,1,0:T(2,128)(2,1)} reshape(bf16[4,8,16,64,128]{4,3,2,1,0:T(8,128)(2,1)} %all_to_all.20) | data formatting | bytes 16777216 | tf_op jit(solution)/shard_map/reshape | solution.py:170
  707.0 15.2 %copy.19 = bf16[4,8,16,64,2,64]{5,3,2,4,1,0:T(8,128)(2,1)} copy(bf16[4,8,16,64,2,64]{5,4,3,2,1,0:T(2,128)(2,1)} %reshape.139) | data formatting | bytes 16777216 | tf_op jit(solution)/shard_map/reshape | solution.py:170
  722.1 22.4 %reshape_reshape.3 = bf16[64,16,8,512]{3,2,1,0:T(8,128)(2,1)} reshape(bf16[4,8,2,16,64,64]{5,4,3,2,1,0:T(8,128)(2,1)} %bitcast.27) | data formatting | bytes 16777216 | tf_op jit(solution)/shard_map/reshape;reshape | solution.py:150
  744.6 11.3 %copy.21 = bf16[64,16,8,512]{3,0,1,2:T(8,128)(2,1)} copy(bf16[64,16,8,512]{3,2,1,0:T(8,128)(2,1)} %reshape_reshape.3) | data formatting | bytes 16777216 | tf_op jit(solution)/shard_map/reshape;reshape | solution.py:150
  755.9 188.7 %all_to_all.21.right = bf16[8,16,64,512]{3,2,1,0:T(8,128)(2,1)S(1)} all-to-all(bf16[8,16,64,512]{3,2,1,0:T(8,128)(2,1)} %bitcast.32), channel_id=1, replica_groups=mesh['band'=8,'grid'=4] {'band'}, dimensions={0} | all-to-all | bytes 16777216 | tf_op jit(solution)/shard_map/all_to_all | solution.py:151
  944.6 13.1 %shard_map.42 = f32[512,512]{1,0:T(8,128)S(1)} custom-call(bf16[8,16,64,512]{3,2,1,0:T(8,128)(2,1)} %all-to-all-done.1.left, bf16[8,16,64,512]{3,2,1,0:T(8,128)(2,1)S(1)} %all_to_all.21.right), custom_call_target="tpu_custom_call" | custom-call | flops 4294967296 | bytes 16777216 | tf_op jit(solution)/shard_map/pallas_call | solution.py:134
  958.8 61.1 %reduce-scatter.2.cloned.1.call-done = f32[64,512]{1,0:T(8,128)} async-done(((f32[512,512]{1,0:T(8,128)}), f32[64,512]{1,0:T(8,128)}) %reduce-scatter.2.cloned.1.call-update) | async-done | bytes 131088 | tf_op jit(solution)/shard_map/reduce_scatter | solution.py:174
  1019.9 22.6 %reshape.140 = bf16[64,16,4096]{2,1,0:T(8,128)(2,1)} reshape(bf16[4,8,2,16,64,64]{5,4,3,2,1,0:T(8,128)(2,1)} %bitcast.28) | data formatting | bytes 16777216 | tf_op jit(solution)/shard_map/reshape | solution.py:171
  1042.4 10.0 all-reduce.5.cloned.1.call-done
  1052.5 1.6 copy.26
  (27 shorter events, 5.6 us)
Async XLA Ops:
  88.5 99.6 %all-to-all-start = ((bf16[4,8,16,64,128]{4,3,2,1,0:T(8,128)(2,1)}), bf16[4,8,16,64,128]{4,3,2,1,0:T(8,128)(2,1)}, u32[]{:S(2)}, u32[]{:S(2)}) async-start(bf16[4,8,16,64,128]{4,3,2,1,0:T(8,128)(2,1)} %reshape.136), calls=%async_computation | async-start | bytes 16777216 | tf_op jit(solution)/shard_map/all_to_all | solution.py:165
  188.1 390.4 %all-to-all-start.1 = ((bf16[8,16,64,512]{3,2,1,0:T(8,128)(2,1)}), bf16[8,16,64,512]{3,2,1,0:T(8,128)(2,1)}, u32[]{:S(2)}, u32[]{:S(2)}) async-start(bf16[8,16,64,512]{3,2,1,0:T(8,128)(2,1)} %bitcast.31), calls=%async_computation.1 | async-start | bytes 16777216 | tf_op jit(solution)/shard_map/all_to_all | solution.py:151
  194.6 222.9 %all-reduce.3.cloned.1.call-start = ((), (), s32[]{:S(2)}) async-start(), calls=%async_computation.5 | async-start | bytes 524288 | tf_op jit(solution)/shard_map/psum | solution.py:19
  197.2 238.5 %all-gather.2.cloned.1.call-start = ((), (), s32[]{:S(2)}) async-start(), calls=%async_computation.6 | async-start | bytes 1310720 | tf_op jit(solution)/shard_map/all_gather | solution.py:161
  419.4 600.5 %reduce-scatter.2.cloned.1.call-start = ((), (), s32[]{:S(2)}) async-start(), calls=%async_computation.7 | async-start | bytes 1179648 | tf_op jit(solution)/shard_map/reduce_scatter | solution.py:174
  435.7 1.2 copy-start
  958.7 93.7 %all-reduce.5.cloned.1.call-start = ((), (), s32[]{:S(2)}) async-start(), calls=%async_computation.8 | async-start | bytes 262144 | tf_op jit(solution)/shard_map/psum | solution.py:175
Sparse Core Ops, SparseCore 0:
  199.3 218.0 all-reduce.2
  419.7 15.9 all-gather.1
  958.8 60.9 reduce-scatter.1
  1022.0 30.3 all-reduce.4
